TPU v7x, 32 devices: a whole 2x2x4 slice. The times are simulated.
32 devices in a mesh: dp: 8 (over z, x), tensor: 4 (over y, core).
Axes of the slice: x: 2, y: 2, z: 4, core: 2. Of those that a mesh axis runs over, the one named last changes fastest.
Arguments:
- tokens: bfloat16 [24576, 512], P(('dp', 'tensor')), may hold values from -6 to 6
- lengths: int32 [16, 4], P('dp'), may hold values from 1 to 768, 1536 in all within a row
- w_qkv: bfloat16 [512, 3, 512], P(None, None, 'tensor'), may hold values from -0.25 to 0.25
- w_out: bfloat16 [512, 512], P('tensor'), may hold values from -1 to 1
- w_up: bfloat16 [512, 2048], P(None, 'tensor'), may hold values from -0.25 to 0.25
- w_down: bfloat16 [2048, 512], P('tensor'), may hold values from -0.125 to 0.125
- w_pool: bfloat16 [1536, 512], replicated, may hold values from -0.15625 to 0.15625
- gain_one: float32 [512], replicated, may hold values from 0.5 to 1.5
- gain_two: float32 [512], replicated, may hold values from 0.5 to 1.5
- pooled_grad: bfloat16 [8192, 512], P(('dp', 'tensor')), may hold values from -6 to 6
Outputs:
- pooled: bfloat16 [8192, 512], P(('dp', 'tensor'))
- rms_block: float32 [], replicated
- rms_pool: float32 [], replicated
- grad_tokens: bfloat16 [24576, 512], P(('dp', 'tensor'))
- grad_qkv: float32 [512, 3, 512], P(None, None, 'tensor')
- grad_out: float32 [512, 512], P('tensor')
- grad_up: float32 [512, 2048], P(None, 'tensor')
- grad_down: float32 [2048, 512], P('tensor')
- grad_pool: float32 [1536, 512], replicated
- grad_gain_one: float32 [512], replicated
- grad_gain_two: float32 [512], replicated
Inputs may be any that keep to these rules, and one draw needn't show every extreme that they name: Each row holds 4 sequences whose lengths sum to 1536; the longest of every row is exactly 768.
All inputs are finite; a program needn't handle non-finite values.
Results may differ from a plain program's by a relative error of at most 0.018.
Values may be sent and summed in bfloat16 or wider, within the bound.
A program may use at most 256 MiB of HBM per device.

v0:
```python
import functools
import math
from types import SimpleNamespace

import jax
import jax.numpy as jnp
import numpy as np
from jax import lax
from jax.experimental import pallas as pl
from jax.experimental.pallas import tpu as pltpu
from jax.sharding import PartitionSpec as P

HEAD = 64
POOL = 3
EPS = 1e-06
BIG = float(2**30)
NEG = -1000000000.0
BLOCK = 256
LEFT = 3
WINDOW = LEFT + 1
CHUNK = 128
F32, BF16 = jnp.float32, jnp.bfloat16
MESH = pl.DeviceIdType.MESH


def dot(a, b, ca=1, cb=0):
    return lax.dot_general(a, b, (((ca,), (cb,)), ((), ())), preferred_element_type=F32)


def part(ref, dim, start, count):
    index = [slice(None)] * len(ref.shape)
    index[dim] = pl.ds(start, count)
    return ref.at[tuple(index)]


def wide(ref, start, count):
    return jnp.concatenate([ref[i, pl.ds(start, count), :] for i in range(ref.shape[0])], axis=1)


def put_wide(ref, start, count, value, stride=None):
    for i in range(ref.shape[0]):
        ref[i, pl.ds(start, count, stride=stride), :] = value[:, i * 128 : (i + 1) * 128]


def on(condition, act):
    if condition is None:
        act()
    else:
        pl.when(condition)(act)


class Links:
    def __init__(self, send, recv, free, partners):
        self.send, self.recv, self.sent, self.partners = send, recv, [], partners
        self.free, self.freed = free, 0

    def copy(self, src, dst, to, sends=None, takes=None):
        k = len(self.sent)
        move = pltpu.make_async_remote_copy(
            src, dst, self.send.at[k], self.recv.at[k], device_id=to, device_id_type=MESH
        )
        on(sends, move.start)
        self.sent.append([move, False, False, sends, takes])
        return k

    def arrived(self, k):
        if not self.sent[k][2]:
            on(self.sent[k][4], self.sent[k][0].wait_recv)
            self.sent[k][2] = True

    def left(self, k):
        if not self.sent[k][1]:
            on(self.sent[k][3], self.sent[k][0].wait_send)
            self.sent[k][1] = True

    def give(self, to, gives=None):
        i = self.freed
        self.freed += 1
        on(gives, lambda: pl.semaphore_signal(self.free.at[i], inc=1, device_id=to, device_id_type=MESH))
        return i

    def granted(self, i, takes=None):
        on(takes, lambda: pl.semaphore_wait(self.free.at[i], 1))

    def finish(self):
        for k in range(len(self.sent)):
            self.left(k)


class Loads:
    def __init__(self, sems):
        self.sems, self.moves = sems, []

    def copy(self, src, dst):
        move = pltpu.make_async_copy(src, dst, self.sems.at[len(self.moves)])
        move.start()
        self.moves.append([move, False])
        return len(self.moves) - 1

    def wait(self, *ks):
        for k in ks:
            if not self.moves[k][1]:
                self.moves[k][0].wait()
                self.moves[k][1] = True

    def finish(self):
        self.wait(*range(len(self.moves)))


class Flow:
    def __init__(self):
        self.gens, self.waits, self.at = {}, {}, 0

    def step(self, name):
        self.waits[name] = next(self.gens[name], None)
        return self.waits[name] is not None

    def start(self, name, gen, held=False):
        self.gens[name] = gen
        self.step(name)

    def release(self, *names):
        pass

    def tick(self):
        for name in PLAN[self.at] if self.at < len(PLAN) else ():
            self.step(name)
        self.at += 1

    def need(self, *names):
        for name in names:
            while self.step(name):
                pass

    def finish(self):
        self.tick()
        live = list(self.gens)
        while live:
            live = [name for name in live if self.step(name)]


def gathered(links, way, shard, buf, dim, size, bit, to_y, to_bit, to_core, owns):
    def rows(ref, start, count):
        return part(ref, dim, pl.multiple_of(start, 16), count)

    near, own = buf.at[1], None
    if way == "y":
        k = links.copy(shard, near, to_y)
        yield (k,)
        if to_core is not None:
            own = links.copy(shard, buf.at[2], to_core)
            owns.append(own)
        links.arrived(k)
        ks = first = ()
    elif len(bit) == 1:
        half = size // 2
        k = links.copy(rows(shard, bit[0] * half, half), rows(near, bit[0] * half, half), to_y)
        yield (k,)
        if to_core is not None:
            own = links.copy(shard, buf.at[2], to_core)
            owns.append(own)
        links.arrived(k)
        piece = rows(near, bit[0] * half, half)
        ks, first = (links.copy(piece, piece, to_bit[0]),), ()
    else:
        quarter = size // 4
        at = (2 * bit[1] + bit[0]) * quarter
        over_x = (2 * bit[1] + 1 - bit[0]) * quarter
        over_z = (2 - 2 * bit[1] + bit[0]) * quarter
        k = links.copy(rows(shard, at, quarter), rows(near, at, quarter), to_y)
        yield (k,)
        if to_core is not None:
            own = links.copy(shard, buf.at[2], to_core)
            owns.append(own)
        links.arrived(k)
        piece = rows(near, at, quarter)
        by_x, by_z = first = links.copy(piece, piece, to_bit[0]), links.copy(piece, piece, to_bit[1])
        yield (by_x, by_z)
        links.arrived(by_x)
        piece = rows(near, over_x, quarter // 2)
        second = links.copy(piece, piece, to_bit[1])
        links.arrived(by_z)
        piece = rows(near, over_z + quarter // 2, quarter // 2)
        ks = (links.copy(piece, piece, to_bit[0]), second)
    if ks:
        yield ks
    for k in ks:
        links.arrived(k)
    if to_core is None:
        for k in ks + first:
            links.left(k)
        return
    k = links.copy(near, buf.at[3], to_core)
    yield (k, own)
    links.arrived(own)
    links.arrived(k)


def reduced(links, loads, acc, dim, base, size, stages, bufs, out, ahead, line):
    lo, n, spans = base, size, []
    two = any(kind == "slot" for kind, _, _ in stages)

    def rows(ref, start, count, slots=False):
        return part(ref, dim + 1 if slots else dim, start if isinstance(start, int) else pl.multiple_of(start, 16), count)

    for (kind, to, bit), buf in zip(stages, bufs):
        if kind == "slot":
            k = links.copy(rows(acc.at[1], lo, n), buf, to)
            acc, two = acc.at[0], False
            mine = rows(acc, lo, n)
        elif kind == "half":
            half = n // 2
            there, here = lo + (1 - bit) * half, lo + bit * half
            if two:
                early = links.copy(rows(acc.at[ahead], there, half), buf.at[ahead], to)
                yield (early,)
                k = links.copy(rows(acc.at[1 - ahead], there, half), buf.at[1 - ahead], to)
            else:
                k = links.copy(rows(acc, there, half), buf, to)
            before = lo
            lo, n = here, half
            mine = rows(acc, lo, n, two)
        elif kind == "line":
            mine, (outer, across) = rows(acc, lo, n), line
            inner = jnp.logical_not(outer)

            def add(mine=mine, buf=buf):
                mine[...] = mine[...] + buf[...]

            k = links.copy(mine, buf, to, outer, inner)
            yield (k,)
            links.arrived(k)
            on(inner, add)
            free = links.give(across, inner)
            links.left(k)
            back = links.give(to, outer)
            links.granted(free, inner)
            k = links.copy(mine, buf, across, inner, inner)
            yield (k,)
            links.arrived(k)
            links.left(k)
            on(inner, add)
            links.granted(back, inner)
            k = links.copy(mine, mine, to, inner, outer)
            yield (k,)
            links.arrived(k)
            continue
        else:
            mine = rows(acc, lo, n)
            k = links.copy(mine, buf, to)
        yield (k,)
        if kind == "half" and two:
            links.arrived(early)
            links.left(early)
        links.arrived(k)
        if kind != "slot":
            links.left(k)
        if kind == "half":
            spans.append((to, before, links.give(to)))
        mine[...] = mine[...] + buf[...]
    for to, before, credit in reversed(spans):
        mine = rows(acc, lo, n)
        links.granted(credit)
        k = links.copy(mine, mine, to)
        yield (k,)
        links.arrived(k)
        lo, n = before, 2 * n
    for i, ref in enumerate(out):
        loads.copy(rows(acc, lo, n) if len(out) == 1 else part(acc.at[i], dim - 1, lo, n), part(ref, 0, lo, n))


def summed(links, terms, bufs, partners):
    for i, to in enumerate(partners):
        k = links.copy(terms.at[i], bufs.at[i], to)
        yield (k,)
        links.arrived(k)
        terms[i + 1] = terms[i] + bufs[i]


ORDER = {
    "d0": ("0yLs", 0, 4),
    "q0": ("1y0s", 0, 2),
    "d3": ("1y0s", 3, 4),
    "p2": ("cY01s", 2, 3),
    "p0": ("c1Y0s", 0, 3),
    "u1": ("y0Ls", 1, 2),
    "q1": ("y0Ls", 1, 2),
    "d1": ("0yLs", 1, 4),
    "p1": ("c0Y1s", 1, 3),
    "d2": ("1y0s", 2, 4),
    "u0": ("10ys", 0, 2),
    "o": ("01ys", 0, 1),
}
WAY = {"wq": "yxz", "wo": "y", "wu": "yxz", "wd": "yxz"}
SLOTS = (2, 0, 3, 1)
PLAN = (
    (), (), (), (), ("wq",), (), (), (), (), (), (), (), (), (), ("wo",), (), ("wo", "wu", "wd",), (), (), (), (),
    (), (), (), (), (), (), (), (), (), (), ("wu",), (), ("wd",), (), ("wu",), (), ("wd",), (), (), (), (), (), (),
    ("d0", "d3", "d1", "d2", "u0",), (), ("d0", "d3", "p2",), ("p0", "d1", "p1", "d2",), (), (), (), (), (), (),
    ("o",), ("u1", "u0",), (), (), ("d0",), (), (), ("p1", "d3", "p0",), (), ("o",), (), (), (), ("d0", "p2",), (),
    (), ("u1", "d1",), ("q0",), ("o", "u0", "d2", "d3", "d0", "p2", "u1", "q1",),
    ("d1", "s", "p1", "u0", "p0", "q0", "d2", "d3", "d0", "o", "s", "p2", "q1", "u1", "p1", "p0", "u0", "d3", "d1",
     "d0", "s", "q0", "d2", "o", "p2", "q1", "u1", "p1", "q0", "d2", "p0", "d3", "u0", "u1", "d1", "s", "p0", "o",
     "p2", "q1", "p1", "u0", "p0", "d1", "q0", "d2", "s", "p2", "o", "p1", "q1", "q0", "o", "u0", "p2", "p2", "p1",
     "p0", "p1", "q1", "p0", "q0",),
)


def stage_kinds(order, bits):
    kinds = []
    for letter in order:
        if letter == "y":
            kinds.append(("slot", 1))
        elif letter in "cY":
            kinds.append(("half", "cY".index(letter)))
        elif letter == "L":
            kinds += [("line", 3)] if bits > 2 else []
        elif letter in "01":
            kinds += [("half", 2 + int(letter))] if int(letter) < bits else []
        else:
            kinds += [("swap", 2 + i) for i in range(3 if "L" in order else 2, bits)]
    return kinds


def buffer_shapes(order, rows, shape, bits):
    kinds, out = stage_kinds(order, bits), []
    two = any(kind == "slot" for kind, _ in kinds)
    for kind, _ in kinds:
        if kind == "slot":
            two = False
        elif kind == "half":
            rows //= 2
        out.append(((2,) if two else ()) + shape(rows))
    return out


def scratch_list(T, D, HC, U, bits):
    L, heads, qb = 2 * T, 2 * HC // HEAD, 2 * T // BLOCK
    blocks = sum(min(i, LEFT) + 1 for i in range(qb))
    kd = POOL * D
    out = [
        ("xb", (T, D), BF16),
        ("nrm", (L, D), BF16),
        ("wq", (2, 3, D, HC), BF16),
        ("wqt", (6 * HC, D), BF16),
        ("wo", (4, HC, D), BF16),
        ("wu", (4, D, U), BF16),
        ("wd", (4, U, D), BF16),
        ("wp", (kd, D), BF16),
        ("pg", (T // POOL, D), BF16),
        ("cos", (HEAD // 2, L), F32),
        ("sin", (HEAD // 2, L), F32),
        ("qxt", (heads, 2 * HEAD, L), BF16),
        ("kt", (heads, HEAD, L), BF16),
        ("vt", (heads, HEAD, L), BF16),
        ("kx", (heads, L, 2 * HEAD), BF16),
        ("vx", (heads, L, 2 * HEAD), BF16),
        ("probs", (heads, blocks * BLOCK, BLOCK), BF16),
        ("rl", (8, L), F32),
        ("ot", (2 * HC, L), BF16),
        ("otf", (4 * HC, T), BF16),
        ("gox", (heads, 2 * HEAD, L), BF16),
        ("gpt", (6 * HC, L), BF16),
        ("h1", (T, D), F32),
        ("h2", (D // 128, T + 8, 128), F32),
        ("g2t", (D // 128, T + 8, 128), F32),
        ("rim", (D // 128, 8, 128), F32),
        ("n2", (T, D), BF16),
        ("act", (T, U), BF16),
        ("gpre", (T, U), BF16),
        ("gn", (T, D), F32),
        ("gatt", (L, D), BF16),
        ("dk", (HEAD, L), F32),
        ("dv", (HEAD, L), F32),
        ("dq", (HEAD, L), F32),
        ("gd", (4, U, D), BF16),
        ("gu", (4, D, U), BF16),
        ("go", (2, HC, D), BF16),
        ("cd", (2, U, D), BF16),
        ("cu", (2, D, U), BF16),
        ("sc0", (WINDOW * BLOCK, BLOCK), F32),
        ("sc1", (WINDOW * BLOCK, BLOCK), F32),
        ("ds0", (WINDOW * BLOCK, BLOCK), BF16),
        ("ds1", (WINDOW * BLOCK, BLOCK), BF16),
        ("terms", (bits + 3, 8, D), F32),
        ("term_in", (bits + 2, 8, D), F32),
    ]
    rows_of = {"d": U, "u": D, "o": HC, "q": D, "p": kd}
    shape_of = {
        "d": lambda n: (n, D),
        "u": lambda n: (n, U),
        "o": lambda n: (n, D),
        "q": lambda n: (3, n, HC),
        "p": lambda n: (n, D),
    }
    for name, (order, _, parts) in ORDER.items():
        shapes = buffer_shapes(order, rows_of[name[0]] // parts, shape_of[name[0]], bits)
        out += [(f"in_{name}_{i}", shape, BF16) for i, shape in enumerate(shapes)]
    return out


def kernel(bits, names, *refs):
    s = SimpleNamespace(**dict(zip(names, refs)))
    T, D = s.xb.shape
    HC, U = s.wo.shape[1], s.wu.shape[2]
    L, QB = 2 * T, 2 * T // BLOCK
    half_head = HEAD // 2
    places, _ = result_rows(T, D, HC, U)
    RC = 32
    loads = Loads(s.load_sems)

    d, t = lax.axis_index("dp"), lax.axis_index("tensor")
    c, y = t % 2, t // 2
    to_core, to_y = (d, t + 1 - 2 * c), (d, t + 2 - 4 * y)
    bit = [(d // (1 << i)) % 2 for i in range(bits)]
    to_bit = [(d + (1 - 2 * bit[i]) * (1 << i), t) for i in range(bits)]
    partners = [to_core, to_y] + to_bit
    outer, across = None, None
    if bits > 2:
        outer = bit[1] == bit[2]
        across = (d + (1 - 2 * bit[1]) * 2 + (1 - 2 * bit[2]) * 4, t)
    links, flow = Links(s.send_sems, s.recv_sems, s.free_sems, partners), Flow()
    sides = [c, y] + bit
    tick = flow.tick

    def start_sum(name, acc, dim, held=False, ahead=1):
        order, piece, parts = ORDER[name]
        size = {"d": U, "u": D, "o": HC, "q": D, "p": POOL * D}[name[0]] // parts
        at, rows = places[name[0]]
        if name[0] == "q":
            out = [s.low_out.at[at : at + rows, i * HC : (i + 1) * HC] for i in range(3)]
        else:
            out = [s.low_out.at[at : at + rows, :]]
        stages = [(kind, partners[i], sides[i]) for kind, i in stage_kinds(order, bits)]
        bufs = [getattr(s, f"in_{name}_{i}") for i in range(len(stages))]
        flow.start(name, reduced(links, loads, acc, dim, piece * size, size, stages, bufs, out, ahead, (outer, across)), held)

    mine = pl.multiple_of(c * T, T)
    theirs = pl.multiple_of((1 - c) * T, T)

    in_x = loads.copy(s.tokens, s.xb)
    in_q = loads.copy(s.w_qkv, s.wq.at[0])
    in_pool = loads.copy(s.w_pool, s.wp)
    in_pg = loads.copy(s.pooled_grad, s.pg)
    in_out = loads.copy(s.w_out, s.wo.at[0])
    in_up = loads.copy(s.w_up, s.wu.at[0])
    in_down = loads.copy(s.w_down, s.wd.at[0])

    barrier = pltpu.get_barrier_semaphore()
    greeted = partners + ([across] if bits > 2 else [])
    for to in greeted:
        pl.semaphore_signal(barrier, inc=1, device_id=to, device_id_type=MESH)
    pl.semaphore_wait(barrier, len(greeted))

    owns = {"wq": [], "wo": [], "wu": [], "wd": []}

    def get(name, shard, buf, dim, size, core):
        flow.start(name, gathered(links, WAY[name], shard, buf, dim, size, bit, to_y, to_bit, core, owns[name]))

    get("wq", s.w_qkv, s.wq, 1, D, None)
    get("wo", s.w_out, s.wo, 0, HC, to_core)
    get("wu", s.w_up, s.wu, 0, D, to_core)
    get("wd", s.w_down, s.wd, 0, U, to_core)

    gain_one, gain_two = s.gain_one[...], s.gain_two[...]
    loads.wait(in_x)
    for r in range(0, T, RC):
        x = s.xb[r : r + RC, :].astype(F32)
        scale = lax.rsqrt(jnp.mean(x * x, axis=1, keepdims=True) + EPS)
        s.nrm[pl.ds(pl.multiple_of(mine + r, RC), RC), :] = (x * scale * gain_one).astype(BF16)
    own_rows = s.nrm.at[pl.ds(mine, T), :]
    sent_norm = links.copy(own_rows, own_rows, to_core)

    starts, ends, total = [], [], 0
    for j in range(4):
        starts.append(total)
        total = total + s.lengths[y, j]
        ends.append(total)

    def kept(j):
        p = mine + POOL * lax.broadcasted_iota(jnp.int32, (T // POOL, 1), 0) + j
        bad = (p - 1) <= 0
        for e in ends[:3]:
            bad = bad | ((p >= e) & (p - 1 <= e))
        return jnp.logical_not(bad)

    loads.wait(in_q)
    cos_in, sin_in = s.angles[2], s.angles[3]
    for i in range(L // 128):
        cos_of, sin_of = s.angles[0, :, i : i + 1], s.angles[1, :, i : i + 1]
        s.cos[:, i * 128 : (i + 1) * 128] = cos_of * cos_in - sin_of * sin_in
        s.sin[:, i * 128 : (i + 1) * 128] = sin_of * cos_in + cos_of * sin_in
    row = lax.broadcasted_iota(jnp.int32, (HEAD, L), 0)
    pos = lax.broadcasted_iota(jnp.int32, (HEAD, L), 1)
    same = jnp.zeros((HEAD, L), F32)
    for j in range(4):
        same = jnp.where((row == j) & (pos >= starts[j]) & (pos < ends[j]), 1.0, same)
    key_rows_doc = same.astype(BF16)
    query_rows_doc = jnp.where(row < 4, BIG * (same - 1.0), 0.0).astype(BF16)
    value_rows = jnp.where(row < 2, -1.0, 0.0).astype(BF16)
    for h in range(4):
        s.qxt[h, HEAD : 2 * HEAD, :] = query_rows_doc

    def turn_weights(slot):
        for i in range(3):
            s.wqt[(3 * slot + i) * HC : (3 * slot + i + 1) * HC, :] = s.wq[slot, i].T

    def project(slot, start):
        for j in range(0, T, BLOCK):
            cols = pl.ds(pl.multiple_of(start + j, BLOCK), BLOCK)
            cosine, sine = s.cos[:, cols], s.sin[:, cols]
            r = dot(s.wqt[3 * slot * HC : 3 * (slot + 1) * HC, :], s.nrm[cols, :], 1, 1)
            for i in range(3):
                for h in range(2):
                    u = r[i * HC + h * HEAD : i * HC + (h + 1) * HEAD, :]
                    head = 2 * slot + h
                    if i == 2:
                        s.vt[head, :, cols] = u.astype(BF16)
                        continue
                    a, b = u[:half_head], u[half_head:]
                    turned = jnp.concatenate([a * cosine - b * sine, a * sine + b * cosine], axis=0)
                    if i == 0:
                        s.qxt[head, 0:HEAD, cols] = (turned * HEAD**-0.5).astype(BF16)
                    else:
                        s.kt[head, :, cols] = turned.astype(BF16)

    def turn_keys(head):
        s.kx[head] = jnp.concatenate([s.kt[head], key_rows_doc], axis=0).T
        s.vx[head] = jnp.concatenate([s.vt[head], value_rows], axis=0).T

    turn_weights(0)
    project(0, mine)
    tick()

    loads.wait(in_pool, in_pg)
    s.g2t[:, 0:8, :] = jnp.zeros((D // 128, 8, 128), F32)
    s.g2t[:, T : T + 8, :] = jnp.zeros((D // 128, 8, 128), F32)
    for j in range(POOL):
        grad_shift = dot(s.pg[...], s.wp[j * D : (j + 1) * D, :], 1, 1)
        put_wide(s.g2t, 8 - (POOL - 1) + j, T // POOL, jnp.where(kept(j), grad_shift, 0.0), POOL)
    sent_rim = links.copy(s.g2t.at[:, 0:8, :], s.rim, to_core)

    tick()
    links.arrived(sent_norm)
    project(0, theirs)
    tick()
    turn_keys(0)
    turn_keys(1)
    tick()

    def window(qb):
        first = max(0, qb - LEFT)
        blocks = qb - first + 1
        offset = sum(min(i, LEFT) + 1 for i in range(qb)) * BLOCK
        return first * BLOCK, blocks, offset, slice(qb * BLOCK, (qb + 1) * BLOCK)

    def score(head, qb, i, into):
        first, blocks, _, q = window(qb)
        rows = slice(i * CHUNK, (i + 1) * CHUNK)
        scores = dot(s.kx[head, first + rows.start : first + rows.stop, :], s.qxt[head, :, q])
        below = rows.start - (blocks - 1) * BLOCK
        if below >= 0:
            ki = lax.broadcasted_iota(jnp.int32, (CHUNK, BLOCK), 0) + below
            qi = lax.broadcasted_iota(jnp.int32, (CHUNK, BLOCK), 1)
            scores = jnp.where(ki <= qi, scores, NEG)
        into[rows, :] = scores
        return jnp.max(scores.reshape(CHUNK // 8, 8, BLOCK), axis=0)

    def attend(head):
        order = list(range(1, QB)) + [0]
        pieces = [window(qb)[1] * BLOCK // CHUNK for qb in order]
        bufs = (s.sc0, s.sc1)
        tops = [score(head, order[0], i, bufs[0]) for i in range(pieces[0])]
        for at, qb in enumerate(order):
            first, blocks, offset, q = window(qb)
            now, later = bufs[at % 2], bufs[(at + 1) % 2]
            top = jnp.max(functools.reduce(jnp.maximum, tops), axis=0, keepdims=True)
            more = pieces[at + 1] if at + 1 < QB else 0
            tops, total = [], jnp.zeros((8, BLOCK), F32)
            for i in range(pieces[at]):
                while len(tops) < (i + 1) * more // pieces[at]:
                    tops.append(score(head, order[at + 1], len(tops), later))
                e = jnp.exp(now[i * CHUNK : (i + 1) * CHUNK, :] - top)
                total = total + jnp.sum(e.reshape(CHUNK // 8, 8, BLOCK), axis=0)
                s.probs[head, offset + i * CHUNK : offset + (i + 1) * CHUNK, :] = e.astype(BF16)
            inverse = 1.0 / jnp.sum(total, axis=0, keepdims=True)
            s.rl[head : head + 1, q] = inverse
            low = s.probs[head, offset : offset + blocks * BLOCK, :]
            out = dot(s.vt[head, :, first : first + blocks * BLOCK], low) * inverse
            s.ot[head * HEAD : (head + 1) * HEAD, q] = out.astype(BF16)
            tick()

    def send_heads(slot):
        rows = slice(slot * HC, (slot + 1) * HC)
        s.otf[rows, :] = s.ot[rows, pl.ds(mine, T)]
        return links.copy(
            s.ot.at[rows, pl.ds(theirs, T)],
            s.otf.at[(2 + slot) * HC : (3 + slot) * HC, :],
            to_core,
        )

    attend(0)
    attend(1)
    sent_heads = [send_heads(0)]
    flow.need("wq")
    turn_weights(1)
    project(1, mine)
    tick()
    project(1, theirs)
    turn_keys(2)
    turn_keys(3)
    tick()
    attend(2)
    attend(3)
    sent_heads.append(send_heads(1))
    tick()
    flow.need("wo")
    loads.wait(in_out)
    for k in sent_heads:
        links.arrived(k)

    for j in range(0, T, BLOCK):
        out = dot(s.otf[:, j : j + BLOCK], s.wo[...].reshape(4 * HC, D), 0, 0)
        for r in range(j, j + BLOCK, RC):
            rows = slice(r, r + RC)
            h = out[r - j : r - j + RC, :] + s.xb[rows, :].astype(F32)
            s.h1[rows, :] = h
            put_wide(s.h2, 8 + r, RC, h)
            scale = lax.rsqrt(jnp.mean(h * h, axis=1, keepdims=True) + EPS)
            s.n2[rows, :] = (h * scale * gain_two).astype(BF16)
    links.arrived(sent_rim)
    tail = lax.broadcasted_iota(jnp.int32, (D // 128, 8, 128), 1) >= 8 - (POOL - 1)
    s.g2t[:, T : T + 8, :] = s.g2t[:, T : T + 8, :] + jnp.where(tail, s.rim[...], 0.0)
    for r in range(0, T, RC):
        branch = wide(s.g2t, 8 + r, RC).astype(BF16)
        s.gatt[pl.ds(pl.multiple_of(mine + r, RC), RC), :] = branch
    tick()
    loads.wait(in_up, in_down)

    root = math.sqrt(2.0 / math.pi)

    def feed_forward(slot, first):
        def one_block(i, carry):
            j = pl.multiple_of(i * BLOCK, BLOCK)
            block, at = pl.ds(j, BLOCK), pl.multiple_of(8 + j, 8)
            v = dot(s.n2[block, :], s.wu[slot])
            grad_act = dot(s.gatt[pl.ds(pl.multiple_of(mine + j, BLOCK), BLOCK), :], s.wd[slot], 1, 1)
            for r in range(0, BLOCK, RC):
                rows = pl.ds(pl.multiple_of(j + r, RC), RC)
                u = v[r : r + RC, :]
                square = u * u
                th = jnp.tanh(u * (root + (root * 0.044715) * square))
                up = 0.5 + 0.5 * th
                slope = up + (u * (up - up * th)) * (root + (root * 3 * 0.044715) * square)
                s.act[rows, :] = (u * up).astype(BF16)
                s.gpre[rows, :] = (grad_act[r : r + RC, :] * slope).astype(BF16)
            put_wide(s.h2, at, BLOCK, wide(s.h2, at, BLOCK) + dot(s.act[block, :], s.wd[slot]))
            grad_normed = dot(s.gpre[block, :], s.wu[slot], 1, 1)
            s.gn[block, :] = grad_normed if first else s.gn[block, :] + grad_normed
            return carry

        lax.fori_loop(0, T // BLOCK, one_block, 0)
        tick()
        branch = s.gatt[pl.ds(mine, T), :]
        for j in range(0, U, BLOCK):
            s.gd[slot, j : j + BLOCK, :] = dot(s.act[:, j : j + BLOCK], branch, 0, 0).astype(BF16)
        tick()
        for j in range(0, D, BLOCK):
            s.gu[slot, j : j + BLOCK, :] = dot(s.n2[:, j : j + BLOCK], s.gpre[...], 0, 0).astype(BF16)
        tick()

    def to_other_core(slot):
        return (
            links.copy(s.gd.at[slot], s.cd.at[slot - 2], to_core),
            links.copy(s.gu.at[slot], s.cu.at[slot - 2], to_core),
        )

    def from_other_core(slot, sent):
        links.arrived(sent[0])
        s.gd[slot] = s.gd[slot] + s.cd[slot]
        links.arrived(sent[1])
        s.gu[slot] = s.gu[slot] + s.cu[slot]

    if SLOTS[0] == 3:
        flow.need("wu", "wd")
    else:
        links.arrived(owns["wu"][0])
        links.arrived(owns["wd"][0])
    shard_sums = {name: s.gd if name[0] == "d" else s.gu for name in ORDER if name[0] in "du"}
    ahead = SLOTS[1]
    early = [name for name in shard_sums if ahead == 1 or ORDER[name][0][0] != "y"]
    feed_forward(SLOTS[0], True)
    sent_one = to_other_core(SLOTS[0])
    feed_forward(SLOTS[1], False)
    from_other_core(SLOTS[1], sent_one)
    for name in early:
        start_sum(name, shard_sums[name].at[0:2], 0, True, ahead)
    flow.need("wu", "wd")
    feed_forward(SLOTS[2], False)
    sent_two = to_other_core(SLOTS[2])
    feed_forward(SLOTS[3], False)

    gain_grad_two = jnp.zeros((8, D), F32)
    for r in range(0, T, RC):
        rows = slice(r, r + RC)
        h, gn = s.h1[rows, :], s.gn[rows, :]
        scale = lax.rsqrt(jnp.mean(h * h, axis=1, keepdims=True) + EPS)
        e = gain_two * gn
        hs = h * scale
        grad = wide(s.g2t, 8 + r, RC) + scale * (e - hs * jnp.mean(e * hs, axis=1, keepdims=True))
        s.h1[rows, :] = grad
        s.gatt[pl.ds(pl.multiple_of(mine + r, RC), RC), :] = grad.astype(BF16)
        gain_grad_two = gain_grad_two + jnp.sum((gn * hs).reshape(RC // 8, 8, D), axis=0)
    own_rows = s.gatt.at[pl.ds(mine, T), :]
    sent_gatt = links.copy(own_rows, own_rows, to_core)
    sent_rim = links.copy(s.h2.at[:, T : T + 8, :], s.h2.at[:, 0:8, :], to_core)
    from_other_core(SLOTS[3], sent_two)
    flow.release(*early)
    for name in shard_sums:
        if name not in early:
            start_sum(name, shard_sums[name].at[0:2], 0)
    tick()

    block_square = jnp.zeros((8, D), F32)
    for r in range(0, T, RC):
        h = wide(s.h2, 8 + r, RC)
        block_square = block_square + jnp.sum((h * h).reshape(RC // 8, 8, D), axis=0)
    links.arrived(sent_rim)
    for j in range(POOL):
        rows = pl.ds(8 - (POOL - 1) + j, T // POOL, stride=POOL)
        taken = jnp.concatenate([s.h2[i, rows, :] for i in range(D // 128)], axis=1)
        s.n2[j * (T // POOL) : (j + 1) * (T // POOL), :] = jnp.where(kept(j), taken, 0.0).astype(BF16)
    pool_in = [s.n2[j * (T // POOL) : (j + 1) * (T // POOL), :] for j in range(POOL)]
    pooled = sum(dot(pool_in[j], s.wp[j * D : (j + 1) * D, :]) for j in range(POOL))
    pool_square = jnp.sum((pooled * pooled).reshape(T // POOL // 8, 8, D), axis=0)
    s.gpre[0 : T // POOL, :] = pooled.astype(BF16)
    out_pooled = loads.copy(s.gpre.at[0 : T // POOL, :], part(s.low_out, 0, *places["pooled"]))
    for j in range(POOL):
        s.wp[j * D : (j + 1) * D, :] = dot(pool_in[j], s.pg[...], 0, 0).astype(BF16)
    for name in (name for name in ORDER if name[0] == "p"):
        start_sum(name, s.wp, 0)
    tick()

    def grad_heads(start):
        for j in range(0, T, BLOCK):
            cols = pl.ds(pl.multiple_of(start + j, BLOCK), BLOCK)
            g = dot(s.wo[0:2].reshape(2 * HC, D), s.gatt[cols, :], 1, 1)
            line = lax.broadcasted_iota(jnp.int32, (HEAD, BLOCK), 0)
            for head in range(4):
                low = (g[head * HEAD : (head + 1) * HEAD] * s.rl[head : head + 1, cols]).astype(BF16)
                o = s.ot[head * HEAD : (head + 1) * HEAD, cols].astype(F32)
                delta = jnp.sum(low.astype(F32) * o, axis=0, keepdims=True)
                high = delta.astype(BF16).astype(F32)
                rest = jnp.where(line == 0, high, jnp.where(line == 1, delta - high, 0.0))
                s.gox[head, 0:HEAD, cols] = low
                s.gox[head, HEAD : 2 * HEAD, cols] = rest.astype(BF16)

    grad_heads(mine)
    links.arrived(sent_gatt)
    grad_heads(theirs)
    for slot in (1, 0):
        s.go[slot] = dot(s.ot[slot * HC : (slot + 1) * HC, :], s.gatt[...]).astype(BF16)
    start_sum("o", s.go, 0)
    tick()

    def grad_score(head, qb, i, into):
        first, _, offset, q = window(qb)
        rows = slice(i * BLOCK, (i + 1) * BLOCK)
        grads = dot(s.vx[head, first + rows.start : first + rows.stop, :], s.gox[head, :, q])
        probs = s.probs[head, offset + rows.start : offset + rows.stop, :]
        into[rows, :] = (probs.astype(F32) * grads).astype(BF16)

    def attend_back(head):
        slot, h = head // 2, head % 2
        bufs, seen = (s.ds0, s.ds1), set()
        for i in range(window(0)[1]):
            grad_score(head, 0, i, bufs[0])
        for qb in range(QB):
            first, blocks, offset, q = window(qb)
            now, later = bufs[qb % 2], bufs[(qb + 1) % 2]
            more, done = window(qb + 1)[1] if qb + 1 < QB else 0, 0
            s.dq[:, q] = dot(s.kt[head, :, first : first + blocks * BLOCK], now[0 : blocks * BLOCK, :])
            for i in range(blocks):
                while done < (i + 1) * more // blocks:
                    grad_score(head, qb + 1, done, later)
                    done += 1
                cols = slice(first + i * BLOCK, first + (i + 1) * BLOCK)
                probs = s.probs[head, offset + i * BLOCK : offset + (i + 1) * BLOCK, :]
                dk = dot(s.qxt[head, 0:HEAD, q], now[i * BLOCK : (i + 1) * BLOCK, :], 1, 1)
                dv = dot(s.gox[head, 0:HEAD, q], probs, 1, 1)
                s.dk[:, cols] = s.dk[:, cols] + dk if cols.start in seen else dk
                s.dv[:, cols] = s.dv[:, cols] + dv if cols.start in seen else dv
                seen.add(cols.start)
            tick()
        cosine, sine = s.cos[...], s.sin[...]
        for i, (ref, factor) in enumerate(((s.dq, HEAD**-0.5), (s.dk, 1.0))):
            a, b = ref[:half_head, :], ref[half_head:, :]
            turned = jnp.concatenate([a * cosine + b * sine, b * cosine - a * sine], axis=0) * factor
            start = (3 * slot + i) * HC + h * HEAD
            s.gpt[start : start + HEAD, :] = turned.astype(BF16)
        start = (3 * slot + 2) * HC + h * HEAD
        s.gpt[start : start + HEAD, :] = s.dv[...].astype(BF16)

    def grad_weights(slot):
        for i in range(3):
            g = dot(s.gpt[(3 * slot + i) * HC : (3 * slot + i + 1) * HC, :], s.nrm[...])
            s.wq[slot, i] = g.astype(BF16).T

    attend_back(2)
    attend_back(3)
    grad_weights(1)
    sums_q = [name for name in ORDER if name[0] == "q"]
    for name in sums_q:
        start_sum(name, s.wq, 1, True)
    attend_back(0)
    attend_back(1)
    grad_weights(0)
    flow.release(*sums_q)
    tick()

    for j in range(0, T, BLOCK):
        cols = pl.ds(pl.multiple_of(theirs + j, BLOCK), BLOCK)
        s.n2[j : j + BLOCK, :] = dot(s.gpt[:, cols], s.wqt[...], 0, 0).astype(BF16)
    sent_pn = links.copy(s.n2, s.act, to_core)
    for j in range(0, T, BLOCK):
        cols = pl.ds(pl.multiple_of(mine + j, BLOCK), BLOCK)
        s.gn[j : j + BLOCK, :] = dot(s.gpt[:, cols], s.wqt[...], 0, 0)
    tick()
    links.arrived(sent_pn)
    loads.wait(out_pooled)
    gain_grad_one = jnp.zeros((8, D), F32)
    for r in range(0, T, RC):
        rows = slice(r, r + RC)
        x, gn = s.xb[rows, :].astype(F32), s.gn[rows, :] + s.act[rows, :].astype(F32)
        scale = lax.rsqrt(jnp.mean(x * x, axis=1, keepdims=True) + EPS)
        e = gain_one * gn
        xs = x * scale
        grad = s.h1[rows, :] + scale * (e - xs * jnp.mean(e * xs, axis=1, keepdims=True))
        s.gpre[rows, :] = grad.astype(BF16)
        gain_grad_one = gain_grad_one + jnp.sum((gn * xs).reshape(RC // 8, 8, D), axis=0)
    loads.copy(s.gpre, part(s.low_out, 0, *places["gtok"]))

    line = lax.broadcasted_iota(jnp.int32, (8, D), 0)
    small = jnp.zeros((8, D), F32)
    for i, v in enumerate((gain_grad_one, gain_grad_two, block_square, pool_square)):
        v = jnp.sum(v, axis=0, keepdims=True)
        if i >= 2:
            v = jnp.sum(v, axis=1, keepdims=True)
        small = jnp.where(line == i, v, small)
    s.terms[0] = small
    flow.start("s", summed(links, s.terms, s.term_in, partners))
    flow.finish()
    loads.copy(s.terms.at[len(partners)], s.small_out)
    links.finish()
    loads.finish()


def result_rows(T, D, HC, U):
    sizes = {"p": POOL * D, "d": U, "u": D, "q": D, "o": HC, "pooled": T // POOL, "gtok": T}
    at, out = 0, {}
    for name, rows in sizes.items():
        out[name] = (at, rows)
        at += rows
    return out, at


def widen(places, block_scale, pool_scale, small, low, *refs):
    rms_block, rms_pool, gain_one, gain_two = refs[:4]
    results, wide_refs, taken, sems = dict(zip(places, refs[4:11])), dict(zip(places, refs[11:16])), refs[16], refs[17]
    loads, ks = Loads(sems), {}
    for name, (at, rows) in places.items():
        ks[name] = loads.copy(low.at[at : at + rows, :], taken.at[at : at + rows, :])
    rms_block[...] = jnp.sqrt(small[2:3, 0:1] * block_scale)
    rms_pool[...] = jnp.sqrt(small[3:4, 0:1] * pool_scale)
    gain_one[...] = small[0:1, :]
    gain_two[...] = small[1:2, :]
    for name, made in wide_refs.items():
        at, rows = places[name]
        loads.wait(ks[name])
        if name == "q":
            for i in range(3):
                width = made.shape[2]
                made[i] = taken[at : at + rows, i * width : (i + 1) * width].astype(F32)
        else:
            made[...] = taken[at : at + rows, :].astype(F32)
        loads.copy(made, results[name])
    for name in ("pooled", "gtok"):
        at, rows = places[name]
        loads.wait(ks[name])
        loads.copy(taken.at[at : at + rows, :], results[name])
    loads.finish()


IN_NAMES = (
    "tokens", "lengths", "w_qkv", "w_out", "w_up", "w_down", "w_pool",
    "gain_one", "gain_two", "pooled_grad", "angles",
)
OUT_NAMES = ("low_out", "small_out")


def tables(length):
    half, lanes = HEAD // 2, 128
    frequency = np.exp(-math.log(10000.0) * np.arange(half) / half)[:, None]
    group = frequency * (lanes * np.minimum(np.arange(lanes), length // lanes))
    within = frequency * np.arange(lanes)
    return np.stack([np.cos(group), np.sin(group), np.cos(within), np.sin(within)]).astype(np.float32)


def shards(tokens, lengths, w_qkv, w_out, w_up, w_down, w_pool, gain_one, gain_two, pooled_grad):
    T, D = tokens.shape
    HC, U = w_out.shape[0], w_up.shape[1]
    dp = lax.axis_size("dp")
    bits = dp.bit_length() - 1
    assert lax.axis_size("tensor") == 4 and lengths.shape == (2, 4) and dp == 1 << bits and bits > 0
    scratch = scratch_list(T, D, HC, U, bits)
    names = IN_NAMES + OUT_NAMES + tuple(n for n, _, _ in scratch) + ("send_sems", "recv_sems", "free_sems", "load_sems")
    hbm, vmem, smem = pl.BlockSpec(memory_space=pl.ANY), pl.BlockSpec(memory_space=pltpu.VMEM), pl.BlockSpec(memory_space=pltpu.SMEM)
    copies = 256 + 24 * bits
    places, total = result_rows(T, D, HC, U)
    low, small = pl.pallas_call(
        functools.partial(kernel, bits, names),
        out_shape=[jax.ShapeDtypeStruct((total, D), BF16), jax.ShapeDtypeStruct((8, D), F32)],
        in_specs=[hbm, smem, hbm, hbm, hbm, hbm, hbm, vmem, vmem, hbm, vmem],
        out_specs=[hbm] * 2,
        scratch_shapes=[pltpu.VMEM(shape, kind) for _, shape, kind in scratch]
        + [pltpu.SemaphoreType.DMA((copies,)), pltpu.SemaphoreType.DMA((copies,))]
        + [pltpu.SemaphoreType.REGULAR((160,)), pltpu.SemaphoreType.DMA((64,))],
        compiler_params=pltpu.CompilerParams(
            collective_id=0, has_side_effects=True, vmem_limit_bytes=64 * 2**20 - 2**16
        ),
    )(
        tokens, lengths, jnp.transpose(w_qkv, (1, 0, 2)), w_out, w_up, w_down, w_pool,
        gain_one.reshape(1, D), gain_two.reshape(1, D), pooled_grad, tables(2 * T),
    )
    group = dp * 4 * T * D
    one, line = jax.ShapeDtypeStruct((1, 1), F32), jax.ShapeDtypeStruct((1, D), F32)
    wide_shapes = [jax.ShapeDtypeStruct(s, F32) for s in ((POOL * D, D), (U, D), (D, U), (3, D, HC), (HC, D))]
    rms_block, rms_pool, grad_one, grad_two, gp, gd, gu, gq, go, pooled, gtok = pl.pallas_call(
        functools.partial(widen, places, 1.0 / group, POOL / group),
        out_shape=[one, one, line, line]
        + wide_shapes
        + [jax.ShapeDtypeStruct((T // POOL, D), BF16), jax.ShapeDtypeStruct((T, D), BF16)],
        in_specs=[vmem, hbm],
        out_specs=[vmem] * 4 + [hbm] * 7,
        scratch_shapes=[pltpu.VMEM(a.shape, F32) for a in wide_shapes]
        + [pltpu.VMEM((total, D), BF16), pltpu.SemaphoreType.DMA((14,))],
        compiler_params=pltpu.CompilerParams(vmem_limit_bytes=62 * 2**20),
    )(small, low)
    return (
        pooled,
        rms_block.reshape(()),
        rms_pool.reshape(()),
        gtok,
        jnp.transpose(gq, (1, 0, 2)),
        go,
        gu,
        gd,
        gp,
        grad_one.reshape(D),
        grad_two.reshape(D),
    )


def solution(mesh):
    rows = P(("dp", "tensor"), None)
    placed = (
        rows, P("dp", None), P(None, None, "tensor"), P("tensor", None), P(None, "tensor"),
        P("tensor", None), P(), P(), P(), rows,
    )
    return jax.shard_map(
        shards,
        mesh=mesh,
        in_specs=placed,
        out_specs=(
            rows, P(), P(), rows, P(None, None, "tensor"), P("tensor", None), P(None, "tensor"),
            P("tensor", None), P(), P(), P(),
        ),
        check_vma=False,
    )
```

profile of v0, /device:TPU:0, one launch (start us, length us, event | category | flops | bytes accessed | tf_op | source)
XLA Modules:
  0.0 111.9 jit_solution(15587021008868991112)
XLA Ops:
  0.6 105.1 %shard_map.194 = (bf16[4224,512]{1,0:T(8,128)(2,1)}, f32[8,512]{1,0:T(8,128)}) custom-call(bf16[768,512]{1,0:T(8,128)(2,1)} %refs_0_.1, s32[2,4]{1,0:T(2,128)} %refs_1_.1, bf16[3,512,128]{2,1,0:T(8,128)(2,1)} %bitcast.8, bf16[128,512]{1,0:T(8,128)(2,1)} %refs_3_.1, bf16[512,512]{1,0:T(8,128)(2,1)} %refs_4_.1, bf16[512,512]{1,0:T(8,128)(2,1)} %refs_5_.1, ...), custom_call_target="tpu_custom_call" | custom-call | tf_op jit(solution)/shard_map/pallas_call | solution.py:920
  105.7 6.0 %shard_map.195 = (f32[1,1]{1,0:T(1,128)}, f32[1,1]{1,0:T(1,128)}, f32[1,512]{1,0:T(1,128)}, f32[1,512]{1,0:T(1,128)}, f32[1536,512]{1,0:T(8,128)}, /*index=5*/f3...) custom-call(f32[8,512]{1,0:T(8,128)} %get-tuple-element.24.small, ...), custom_call_target="tpu_custom_call" | custom-call | tf_op jit(solution)/shard_map/pallas_call | solution.py:938
where the time goes:
time: 112 us
  Pallas kernels  111 us (99%)
    pallas_call x1, Pallas kernels, shards(): pl.pallas_call(functools.partial(kernel, bits, names), out_shape=[jax.Sha...  105 us
    pallas_call x1, Pallas kernels, shards(): pl.pallas_call(functools.partial(widen, places, 1.0 / group, POOL / group...  6.01 us

commit v1 on v0

--- a/solution.py
+++ b/solution.py
@@ -279,30 +279,32 @@
 
 ORDER = {
     "d0": ("0yLs", 0, 4),
+    "d1": ("0yLs", 1, 4),
+    "d2": ("1y0s", 2, 4),
+    "d3": ("1y0s", 3, 4),
+    "u0": ("1y0s", 0, 4),
+    "u1": ("0yLs", 1, 4),
+    "u2": ("1y0s", 2, 4),
+    "u3": ("y0Ls", 3, 4),
+    "p0": ("c1Y0s", 0, 3),
+    "p1": ("c0YLs", 1, 3),
+    "p2": ("cY01s", 2, 3),
+    "o": ("0yLs", 0, 1),
     "q0": ("1y0s", 0, 2),
-    "d3": ("1y0s", 3, 4),
-    "p2": ("cY01s", 2, 3),
-    "p0": ("c1Y0s", 0, 3),
-    "u1": ("y0Ls", 1, 2),
     "q1": ("y0Ls", 1, 2),
-    "d1": ("0yLs", 1, 4),
-    "p1": ("c0Y1s", 1, 3),
-    "d2": ("1y0s", 2, 4),
-    "u0": ("10ys", 0, 2),
-    "o": ("01ys", 0, 1),
 }
 WAY = {"wq": "yxz", "wo": "y", "wu": "yxz", "wd": "yxz"}
 SLOTS = (2, 0, 3, 1)
 PLAN = (
     (), (), (), (), ("wq",), (), (), (), (), (), (), (), (), (), ("wo",), (), ("wo", "wu", "wd",), (), (), (), (),
     (), (), (), (), (), (), (), (), (), (), ("wu",), (), ("wd",), (), ("wu",), (), ("wd",), (), (), (), (), (), (),
-    ("d0", "d3", "d1", "d2", "u0",), (), ("d0", "d3", "p2",), ("p0", "d1", "p1", "d2",), (), (), (), (), (), (),
-    ("o",), ("u1", "u0",), (), (), ("d0",), (), (), ("p1", "d3", "p0",), (), ("o",), (), (), (), ("d0", "p2",), (),
-    (), ("u1", "d1",), ("q0",), ("o", "u0", "d2", "d3", "d0", "p2", "u1", "q1",),
-    ("d1", "s", "p1", "u0", "p0", "q0", "d2", "d3", "d0", "o", "s", "p2", "q1", "u1", "p1", "p0", "u0", "d3", "d1",
-     "d0", "s", "q0", "d2", "o", "p2", "q1", "u1", "p1", "q0", "d2", "p0", "d3", "u0", "u1", "d1", "s", "p0", "o",
-     "p2", "q1", "p1", "u0", "p0", "d1", "q0", "d2", "s", "p2", "o", "p1", "q1", "q0", "o", "u0", "p2", "p2", "p1",
-     "p0", "p1", "q1", "p0", "q0",),
+    ("d0", "d2", "d1", "d3", "u0", "u1", "u2",), (), ("d0", "d2", "p0",), ("p1", "u3", "d1", "p2", "d3",), (), (),
+    ("u1", "u0",), (), ("d0", "o", "u2",), (), (), ("d2",), (), (), ("d1", "p1", "p0",), (), (), ("u3", "d0",), (),
+    ("p2", "o",), ("d2", "d1", "d3",), (), (), (), ("u1", "d0",), (), ("p2", "u0", "d3", "u3",), ("q0", "d2", "u2",),
+    ("d1", "u1", "d0", "p1", "u0", "p2", "p0", "d2", "d3", "u2", "u3", "q0",),
+    ("s", "q1", "d1", "u1", "d0", "p1", "o", "p0", "d3", "u0", "q0", "d2", "s", "p2", "q1", "u3", "u2", "o", "d1",
+     "p1", "u0", "u1", "q0", "s", "p0", "d3", "u3", "p2", "o", "u2", "q1", "p1", "u1", "p0", "u0", "q0", "p2", "s",
+     "p1", "o", "q1", "p0", "q0", "u2", "s", "p2", "q1", "p1", "p2", "p1", "o", "p0", "p0", "q1", "q0",),
 )
 
 
@@ -867,27 +869,30 @@
 def widen(places, block_scale, pool_scale, small, low, *refs):
     rms_block, rms_pool, gain_one, gain_two = refs[:4]
     results, wide_refs, taken, sems = dict(zip(places, refs[4:11])), dict(zip(places, refs[11:16])), refs[16], refs[17]
-    loads, ks = Loads(sems), {}
+    loads, pieces = Loads(sems), []
     for name, (at, rows) in places.items():
-        ks[name] = loads.copy(low.at[at : at + rows, :], taken.at[at : at + rows, :])
+        cut = rows // POOL if name == "p" else rows
+        for first in range(0, rows, cut):
+            place = slice(at + first, at + first + cut)
+            pieces.append((name, slice(first, first + cut), place, loads.copy(low.at[place, :], taken.at[place, :])))
     rms_block[...] = jnp.sqrt(small[2:3, 0:1] * block_scale)
     rms_pool[...] = jnp.sqrt(small[3:4, 0:1] * pool_scale)
     gain_one[...] = small[0:1, :]
     gain_two[...] = small[1:2, :]
-    for name, made in wide_refs.items():
-        at, rows = places[name]
-        loads.wait(ks[name])
+    for name, rows, place, k in pieces:
+        loads.wait(k)
+        if name not in wide_refs:
+            loads.copy(taken.at[place, :], results[name])
+            continue
+        made = wide_refs[name]
         if name == "q":
             for i in range(3):
                 width = made.shape[2]
-                made[i] = taken[at : at + rows, i * width : (i + 1) * width].astype(F32)
+                made[i] = taken[place, i * width : (i + 1) * width].astype(F32)
+            loads.copy(made, results[name])
         else:
-            made[...] = taken[at : at + rows, :].astype(F32)
-        loads.copy(made, results[name])
-    for name in ("pooled", "gtok"):
-        at, rows = places[name]
-        loads.wait(ks[name])
-        loads.copy(taken.at[at : at + rows, :], results[name])
+            made[rows, :] = taken[place, :].astype(F32)
+            loads.copy(made.at[rows, :], results[name].at[rows, :])
     loads.finish()
 
 
@@ -943,7 +948,7 @@
         in_specs=[vmem, hbm],
         out_specs=[vmem] * 4 + [hbm] * 7,
         scratch_shapes=[pltpu.VMEM(a.shape, F32) for a in wide_shapes]
-        + [pltpu.VMEM((total, D), BF16), pltpu.SemaphoreType.DMA((14,))],
+        + [pltpu.VMEM((total, D), BF16), pltpu.SemaphoreType.DMA((18,))],
         compiler_params=pltpu.CompilerParams(vmem_limit_bytes=62 * 2**20),
     )(small, low)
     return (

time: 112 us -> 108 us (0.964)
  Pallas kernels: 111 us -> 107 us
    pallas_call x1, Pallas kernels: 105 us -> 101 us  [shards(): pl.pallas_call(functools.partial(kernel, bits, names), out_shape=[jax.Sha...]
where the time goes in v1:
time: 108 us
  Pallas kernels  107 us (99%)
    pallas_call x1, Pallas kernels, shards(): pl.pallas_call(functools.partial(kernel, bits, names), out_shape=[jax.Sha...  101 us
    pallas_call x1, Pallas kernels, shards(): pl.pallas_call(functools.partial(widen, places, 1.0 / group, POOL / group...  5.55 us

profile of v1, /device:TPU:0, one launch (start us, length us, event | category | flops | bytes accessed | tf_op | source)
XLA Modules:
  0.0 107.8 jit_solution(4786249110536553484)
XLA Ops:
  0.6 101.4 %shard_map.194 = (bf16[4224,512]{1,0:T(8,128)(2,1)}, f32[8,512]{1,0:T(8,128)}) custom-call(bf16[768,512]{1,0:T(8,128)(2,1)} %refs_0_.1, s32[2,4]{1,0:T(2,128)} %refs_1_.1, bf16[3,512,128]{2,1,0:T(8,128)(2,1)} %bitcast.8, bf16[128,512]{1,0:T(8,128)(2,1)} %refs_3_.1, bf16[512,512]{1,0:T(8,128)(2,1)} %refs_4_.1, bf16[512,512]{1,0:T(8,128)(2,1)} %refs_5_.1, ...), custom_call_target="tpu_custom_call" | custom-call | tf_op jit(solution)/shard_map/pallas_call | solution.py:925
  102.1 5.5 %shard_map.195 = (f32[1,1]{1,0:T(1,128)}, f32[1,1]{1,0:T(1,128)}, f32[1,512]{1,0:T(1,128)}, f32[1,512]{1,0:T(1,128)}, f32[1536,512]{1,0:T(8,128)}, /*index=5*/f3...) custom-call(f32[8,512]{1,0:T(8,128)} %get-tuple-element.24.small, ...), custom_call_target="tpu_custom_call" | custom-call | tf_op jit(solution)/shard_map/pallas_call | solution.py:943

commit v2 on v1

--- a/solution.py
+++ b/solution.py
@@ -18,6 +18,7 @@
 BLOCK = 256
 LEFT = 3
 WINDOW = LEFT + 1
+FEED = 384
 CHUNK = 128
 F32, BF16 = jnp.float32, jnp.bfloat16
 MESH = pl.DeviceIdType.MESH
@@ -643,11 +644,11 @@
 
     def feed_forward(slot, first):
         def one_block(i, carry):
-            j = pl.multiple_of(i * BLOCK, BLOCK)
-            block, at = pl.ds(j, BLOCK), pl.multiple_of(8 + j, 8)
+            j = pl.multiple_of(i * FEED, FEED)
+            block, at = pl.ds(j, FEED), pl.multiple_of(8 + j, 8)
             v = dot(s.n2[block, :], s.wu[slot])
-            grad_act = dot(s.gatt[pl.ds(pl.multiple_of(mine + j, BLOCK), BLOCK), :], s.wd[slot], 1, 1)
-            for r in range(0, BLOCK, RC):
+            grad_act = dot(s.gatt[pl.ds(pl.multiple_of(mine + j, FEED), FEED), :], s.wd[slot], 1, 1)
+            for r in range(0, FEED, RC):
                 rows = pl.ds(pl.multiple_of(j + r, RC), RC)
                 u = v[r : r + RC, :]
                 square = u * u
@@ -656,12 +657,12 @@
                 slope = up + (u * (up - up * th)) * (root + (root * 3 * 0.044715) * square)
                 s.act[rows, :] = (u * up).astype(BF16)
                 s.gpre[rows, :] = (grad_act[r : r + RC, :] * slope).astype(BF16)
-            put_wide(s.h2, at, BLOCK, wide(s.h2, at, BLOCK) + dot(s.act[block, :], s.wd[slot]))
+            put_wide(s.h2, at, FEED, wide(s.h2, at, FEED) + dot(s.act[block, :], s.wd[slot]))
             grad_normed = dot(s.gpre[block, :], s.wu[slot], 1, 1)
             s.gn[block, :] = grad_normed if first else s.gn[block, :] + grad_normed
             return carry
 
-        lax.fori_loop(0, T // BLOCK, one_block, 0)
+        lax.fori_loop(0, T // FEED, one_block, 0)
         tick()
         branch = s.gatt[pl.ds(mine, T), :]
         for j in range(0, U, BLOCK):
@@ -820,26 +821,35 @@
     flow.release(*sums_q)
     tick()
 
-    for j in range(0, T, BLOCK):
-        cols = pl.ds(pl.multiple_of(theirs + j, BLOCK), BLOCK)
-        s.n2[j : j + BLOCK, :] = dot(s.gpt[:, cols], s.wqt[...], 0, 0).astype(BF16)
+    def partial_normed(into, start):
+        def one_block(i, carry):
+            j = pl.multiple_of(i * BLOCK, BLOCK)
+            cols = pl.ds(pl.multiple_of(start + j, BLOCK), BLOCK)
+            into[pl.ds(j, BLOCK), :] = dot(s.gpt[:, cols], s.wqt[...], 0, 0).astype(into.dtype)
+            return carry
+
+        lax.fori_loop(0, T // BLOCK, one_block, 0)
+
+    partial_normed(s.n2, theirs)
     sent_pn = links.copy(s.n2, s.act, to_core)
-    for j in range(0, T, BLOCK):
-        cols = pl.ds(pl.multiple_of(mine + j, BLOCK), BLOCK)
-        s.gn[j : j + BLOCK, :] = dot(s.gpt[:, cols], s.wqt[...], 0, 0)
+    partial_normed(s.gn, mine)
     tick()
     links.arrived(sent_pn)
     loads.wait(out_pooled)
-    gain_grad_one = jnp.zeros((8, D), F32)
-    for r in range(0, T, RC):
-        rows = slice(r, r + RC)
-        x, gn = s.xb[rows, :].astype(F32), s.gn[rows, :] + s.act[rows, :].astype(F32)
-        scale = lax.rsqrt(jnp.mean(x * x, axis=1, keepdims=True) + EPS)
-        e = gain_one * gn
-        xs = x * scale
-        grad = s.h1[rows, :] + scale * (e - xs * jnp.mean(e * xs, axis=1, keepdims=True))
-        s.gpre[rows, :] = grad.astype(BF16)
-        gain_grad_one = gain_grad_one + jnp.sum((gn * xs).reshape(RC // 8, 8, D), axis=0)
+
+    def norm_back(i, total):
+        for r in range(0, BLOCK, RC):
+            rows = pl.ds(pl.multiple_of(i * BLOCK + r, RC), RC)
+            x, gn = s.xb[rows, :].astype(F32), s.gn[rows, :] + s.act[rows, :].astype(F32)
+            scale = lax.rsqrt(jnp.mean(x * x, axis=1, keepdims=True) + EPS)
+            e = gain_one * gn
+            xs = x * scale
+            grad = s.h1[rows, :] + scale * (e - xs * jnp.mean(e * xs, axis=1, keepdims=True))
+            s.gpre[rows, :] = grad.astype(BF16)
+            total = total + jnp.sum((gn * xs).reshape(RC // 8, 8, D), axis=0)
+        return total
+
+    gain_grad_one = lax.fori_loop(0, T // BLOCK, norm_back, jnp.zeros((8, D), F32))
     loads.copy(s.gpre, part(s.low_out, 0, *places["gtok"]))
 
     line = lax.broadcasted_iota(jnp.int32, (8, D), 0)

time: 108 us -> 107 us (level)
  no operation moved by 1% of the time
where the time goes in v2:
time: 107 us
  Pallas kernels  106 us (99%)
    pallas_call x1, Pallas kernels, shards(): pl.pallas_call(functools.partial(kernel, bits, names), out_shape=[jax.Sha...  100 us
    pallas_call x1, Pallas kernels, shards(): pl.pallas_call(functools.partial(widen, places, 1.0 / group, POOL / group...  5.55 us

profile of v2, /device:TPU:0, one launch (start us, length us, event | category | flops | bytes accessed | tf_op | source)
XLA Modules:
  0.0 106.8 jit_solution(5628630213374078556)
XLA Ops:
  0.6 100.4 %shard_map.194 = (bf16[4224,512]{1,0:T(8,128)(2,1)}, f32[8,512]{1,0:T(8,128)}) custom-call(bf16[768,512]{1,0:T(8,128)(2,1)} %refs_0_.1, s32[2,4]{1,0:T(2,128)} %refs_1_.1, bf16[3,512,128]{2,1,0:T(8,128)(2,1)} %bitcast.8, bf16[128,512]{1,0:T(8,128)(2,1)} %refs_3_.1, bf16[512,512]{1,0:T(8,128)(2,1)} %refs_4_.1, bf16[512,512]{1,0:T(8,128)(2,1)} %refs_5_.1, ...), custom_call_target="tpu_custom_call" | custom-call | tf_op jit(solution)/shard_map/pallas_call | solution.py:935
  101.0 5.5 %shard_map.195 = (f32[1,1]{1,0:T(1,128)}, f32[1,1]{1,0:T(1,128)}, f32[1,512]{1,0:T(1,128)}, f32[1,512]{1,0:T(1,128)}, f32[1536,512]{1,0:T(8,128)}, /*index=5*/f3...) custom-call(f32[8,512]{1,0:T(8,128)} %get-tuple-element.24.small, ...), custom_call_target="tpu_custom_call" | custom-call | tf_op jit(solution)/shard_map/pallas_call | solution.py:953
